TPU v7x, 512 devices: a whole 4x8x8 slice. The times are simulated.
512 devices in a mesh: dp: 16 (over z, core), expert: 32 (over y, x).
Axes of the slice: x: 4, y: 8, z: 8, core: 2. Of those that a mesh axis runs over, the one named last changes fastest.
Arguments:
- tokens: bfloat16 [4096, 2048], P(('dp', 'expert')), may hold values from -6 to 6
- grad_out: bfloat16 [4096, 2048], P(('dp', 'expert')), may hold values from -6 to 6
- gate_weights: bfloat16 [4096, 4], P(('dp', 'expert')), may hold values from 0.049804688 to 0.59765625
- expert_ids: int32 [4096, 4], P(('dp', 'expert')), may hold values from 0 to 31, all different within a row; in each aligned block of 8 rows (0 to 7, 8 to 15, ...) at most 2 rows name the same one
- w_gate: bfloat16 [32, 2048, 2048], P('expert', None, 'dp'), may hold values from -0.125 to 0.125
- w_up: bfloat16 [32, 2048, 2048], P('expert', None, 'dp'), may hold values from -0.125 to 0.125
- w_down: bfloat16 [32, 2048, 2048], P('expert', 'dp'), may hold values from -0.125 to 0.125
Outputs:
- grad_tokens: bfloat16 [4096, 2048], P(('dp', 'expert'))
- grad_w_gate: float32 [32, 2048, 2048], P('expert', None, 'dp')
- grad_w_up: float32 [32, 2048, 2048], P('expert', None, 'dp')
- grad_w_down: float32 [32, 2048, 2048], P('expert', 'dp')
Inputs may be any that keep to these rules, and one draw needn't show every extreme that they name: `expert_ids`: each row names 4 different experts. Among the 8 rows of one device no expert is named more than 2 times, and in every draw some expert is named exactly 2 times by the rows of some device.
All inputs are finite; a program needn't handle non-finite values.
Results may differ from a plain program's by a relative error of at most 0.024.
Values may be sent and summed in bfloat16 or wider, within the bound.
A program may use at most 64 MiB of HBM per device.

v0:
```python
import jax
import jax.numpy as jnp
from jax import lax
from jax.sharding import PartitionSpec as P


def slot_table(expert_ids, gate_weights, experts, capacity):
    token_rows = expert_ids.shape[0]
    top_count = expert_ids.shape[1]
    assignments = token_rows * top_count
    flat_ids = expert_ids.reshape(assignments)
    position = jnp.arange(assignments, dtype=jnp.int32)
    earlier = (flat_ids[None, :] == flat_ids[:, None]) & (position[None, :] < position[:, None])
    rank_of = jnp.sum(earlier.astype(jnp.int32), axis=1)
    places = flat_ids * capacity + rank_of
    columns = jnp.arange(experts * capacity, dtype=jnp.int32)
    picked = (places[:, None] == columns[None, :]).astype(jnp.float32)
    weighted = picked * gate_weights.reshape(assignments, 1).astype(jnp.float32)
    return jnp.sum(weighted.reshape(token_rows, top_count, experts * capacity), axis=1).astype(
        jnp.bfloat16
    )


def on_device(tokens, grad_out, gate_weights, expert_ids, w_gate, w_up, w_down):
    token_rows = tokens.shape[0]
    model_width = tokens.shape[1]
    experts = lax.axis_size("expert")
    capacity = max(2, 2 * token_rows * expert_ids.shape[1] // experts)
    slot_count = experts * capacity
    weights_of = slot_table(expert_ids, gate_weights, experts, capacity)
    member = (weights_of != 0).astype(jnp.bfloat16)
    x_slots = jnp.einsum("tp,td->pd", member, tokens, preferred_element_type=jnp.float32).astype(
        jnp.bfloat16
    )
    scaled_slots = jnp.einsum(
        "tp,td->pd", weights_of, grad_out, preferred_element_type=jnp.float32
    ).astype(jnp.bfloat16)
    arrived = (
        lax.all_to_all(
            x_slots.reshape(experts, capacity, model_width),
            "expert",
            split_axis=0,
            concat_axis=0,
            tiled=True,
        ),
        lax.all_to_all(
            scaled_slots.reshape(experts, capacity, model_width),
            "expert",
            split_axis=0,
            concat_axis=0,
            tiled=True,
        ),
    )
    column = (
        lax.all_gather(arrived[0].reshape(1, slot_count, model_width), "dp", axis=0, tiled=True),
        lax.all_gather(arrived[1].reshape(1, slot_count, model_width), "dp", axis=0, tiled=True),
    )
    routed_rows = column[0].reshape(-1, model_width)
    scaled = column[1].reshape(-1, model_width)
    gate_block = w_gate[0]
    hidden_units = gate_block.shape[1]
    stacked = jnp.concatenate([gate_block, w_up[0]], axis=1)
    down_block = w_down[0]
    pre_both = jnp.dot(routed_rows, stacked, preferred_element_type=jnp.float32)
    gate_pre = pre_both[:, :hidden_units]
    up_pre = pre_both[:, hidden_units:]
    logistic = jax.nn.sigmoid(gate_pre)
    activated = gate_pre * logistic
    hidden = (activated * up_pre).astype(jnp.bfloat16)
    grad_hidden = lax.dot_general(
        scaled, down_block, (((1,), (1,)), ((), ())), preferred_element_type=jnp.float32
    )
    grad_up = (grad_hidden * activated).astype(jnp.bfloat16)
    grad_gate = (grad_hidden * up_pre * (logistic * (1.0 + gate_pre * (1.0 - logistic)))).astype(
        jnp.bfloat16
    )
    hidden_grads = jnp.concatenate([grad_gate, grad_up], axis=1)
    first_grads = lax.dot_general(
        routed_rows, hidden_grads, (((0,), (0,)), ((), ())), preferred_element_type=jnp.float32
    )
    down_grads = lax.dot_general(
        hidden, scaled, (((0,), (0,)), ((), ())), preferred_element_type=jnp.float32
    )
    summed = lax.psum_scatter(
        lax.dot_general(
            hidden_grads, stacked, (((1,), (1,)), ((), ())), preferred_element_type=jnp.float32
        ).astype(jnp.bfloat16),
        "dp",
        scatter_dimension=0,
        tiled=True,
    )
    returned = lax.all_to_all(
        summed.reshape(experts, capacity, model_width),
        "expert",
        split_axis=0,
        concat_axis=0,
        tiled=True,
    )
    grad_tokens = jnp.einsum(
        "tp,pd->td",
        member,
        returned.reshape(slot_count, model_width),
        preferred_element_type=jnp.float32,
    ).astype(jnp.bfloat16)
    return (
        grad_tokens,
        first_grads[:, :hidden_units][None],
        first_grads[:, hidden_units:][None],
        down_grads[None],
    )


def solution(mesh):
    placed = (
        P(("dp", "expert"), None),
        P(("dp", "expert"), None),
        P(("dp", "expert"), None),
        P(("dp", "expert"), None),
        P("expert", None, "dp"),
        P("expert", None, "dp"),
        P("expert", "dp", None),
    )
    return jax.shard_map(
        on_device,
        mesh=mesh,
        in_specs=placed,
        out_specs=(
            P(("dp", "expert"), None),
            P("expert", None, "dp"),
            P("expert", None, "dp"),
            P("expert", "dp", None),
        ),
        check_vma=False,
    )
```

profile of v0, /device:TPU:1, one launch (start us, length us, event | category | flops | bytes accessed | tf_op | source)
XLA Modules:
  0.0 223.2 jit_solution(1614458574236394785)
XLA Ops:
  7.2 0.0 copy-start
  7.2 0.0 copy-start.1
  7.2 0.0 copy-start.2
  7.2 0.0 all-gather.5.cloned.1.call-start
  7.2 0.8 convert_element_type.38
  8.0 0.8 copy.20
  8.8 0.1 eq.29
  8.9 0.2 convert_reduce_fusion
  9.1 0.1 reduce_sum.21
  9.1 0.1 copy.22
  9.2 0.1 select_reduce_fusion
  9.3 1.0 convolution_convert_fusion.1
  10.4 0.2 reshape.67
  10.5 21.5 %all_to_all.15 = bf16[32,2,2048]{2,1,0:T(2,128)(2,1)S(1)} all-to-all(bf16[32,2,2048]{2,1,0:T(2,128)(2,1)S(1)} %reshape.67), channel_id=1, replica_groups=mesh['dp'=16,'expert'=32] {'expert'}, dimensions={0} | all-to-all | bytes 524288 | tf_op jit(solution)/shard_map/all_to_all | solution.py:39
  32.0 0.8 reshape.68
  32.8 0.0 all-gather.5.cloned.1.call-update
  32.9 0.0 all-gather.3.cloned.1.call-start
  32.9 1.0 convolution_convert_fusion.2
  33.9 0.2 reshape.64
  34.1 15.0 %all_to_all.16 = bf16[32,2,2048]{2,1,0:T(2,128)(2,1)S(1)} all-to-all(bf16[32,2,2048]{2,1,0:T(2,128)(2,1)S(1)} %reshape.64), channel_id=1, replica_groups=mesh['dp'=16,'expert'=32] {'expert'}, dimensions={0} | all-to-all | bytes 524288 | tf_op jit(solution)/shard_map/all_to_all | solution.py:46
  49.1 0.8 reshape.65
  49.9 0.0 all-gather.3.cloned.1.call-update
  49.9 0.0 reduce-scatter.2.cloned.1.call-start
  50.0 29.8 %all-gather.5.cloned.1.call-done = bf16[16,64,2048]{2,1,0:T(8,128)(2,1)} async-done(((bf16[1,64,2048]{2,1,0:T(8,128)(2,1)}), bf16[16,64,2048]{2,1,0:T(8,128)(2,1)}) %all-gather.5.cloned.1.call-update) | async-done | bytes 4194320 | tf_op jit(solution)/shard_map/all_gather | solution.py:55
  79.7 0.0 copy-done.1
  79.7 0.0 copy-done.2
  79.7 4.5 %fusion = f32[1024,256]{0,1:T(8,128)} fusion(bf16[1024,2048]{1,0:T(8,128)(2,1)} %bitcast.27, bf16[2048,128]{1,0:T(8,128)(2,1)S(1)} %bitcast.23, bf16[2048,128]{1,0:T(8,128)(2,1)S(1)} %bitcast.25), kind=kOutput, calls=%fused_computation.8 | convolution fusion | flops 1075838976 | bytes 6291456 | tf_op jit(solution)/shard_map/dot_general | solution.py:64
  84.2 42.0 %all-gather.3.cloned.1.call-done = bf16[16,64,2048]{2,1,0:T(8,128)(2,1)} async-done(((bf16[1,64,2048]{2,1,0:T(8,128)(2,1)}), bf16[16,64,2048]{2,1,0:T(8,128)(2,1)}) %all-gather.3.cloned.1.call-update) | async-done | bytes 4194320 | tf_op jit(solution)/shard_map/all_gather | solution.py:56
  126.2 0.0 copy-done
  126.2 4.0 %multiply_convert_fusion.2 = (bf16[1024,128]{0,1:T(8,128)(2,1)S(1)}, bf16[1024,128]{0,1:T(8,128)(2,1)S(1)}) fusion(f32[1024,256]{0,1:T(8,128)} %fusion, bf16[1024,2048]{1,0:T(8,128)(2,1)} %bitcast.29, bf16[1,128,2048]{2,1,0:T(8,128)(2,1)S(1)} %copy-done), kind=kOutput, calls=%fused_computation.14 | convolution fusion | flops 538574848 | bytes 6291456 | tf_op jit(solution)/shard_map/dot_general | solution.py:70
  130.3 3.3 %convolution_convert_fusion = bf16[1024,2048]{1,0:T(8,128)(2,1)} fusion(bf16[2048,128]{1,0:T(8,128)(2,1)S(1)} %bitcast.24, bf16[2048,128]{1,0:T(8,128)(2,1)S(1)} %bitcast.26, bf16[1024,128]{0,1:T(8,128)(2,1)S(1)} %get-tuple-element.7, bf16[1024,128]{0,1:T(8,128)(2,1)S(1)} %get-tuple-element.6), kind=kOutput, calls=%fused_computation | convolution fusion | flops 1078984704 | bytes 5767168 | tf_op jit(solution)/shard_map/dot_general | solution.py:85
  133.6 0.0 copy-start.4
  133.6 0.0 reduce-scatter.2.cloned.1.call-update
  133.6 1.2 copy-done.4
  134.8 0.0 copy-start.3
  134.8 4.1 %convolution_bitcast_fusion = f32[1,128,2048]{2,1,0:T(8,128)} fusion(bf16[1024,2048]{1,0:T(8,128)(2,1)} %bitcast.30, f32[1024,256]{0,1:T(8,128)S(1)} %copy-done.4), kind=kOutput, calls=%fused_computation.1 | convolution fusion | flops 537657344 | bytes 6291456 | tf_op jit(solution)/shard_map/dot_general | solution.py:81
  138.8 0.0 copy-done.3
  138.8 1.4 fusion.4
  140.2 54.4 %reduce-scatter.2.cloned.1.call-done = bf16[64,2048]{1,0:T(8,128)(2,1)} async-done(((bf16[1024,2048]{1,0:T(8,128)(2,1)}), bf16[64,2048]{1,0:T(8,128)(2,1)}) %reduce-scatter.2.cloned.1.call-update) | async-done | bytes 262160 | tf_op jit(solution)/shard_map/reduce_scatter | solution.py:84
  194.6 1.8 reshape.70
  196.5 8.9 %all-to-all-start.2 = ((bf16[32,2,2048]{2,1,0:T(2,128)(2,1)}), bf16[32,2,2048]{2,1,0:T(2,128)(2,1)S(1)}, u32[]{:S(2)}, u32[]{:S(2)}) async-start(bf16[32,2,2048]{2,1,0:T(2,128)(2,1)} %reshape.70), calls=%async_computation.3 | async-start | bytes 524288 | tf_op jit(solution)/shard_map/all_to_all | solution.py:92
  205.4 1.5 slice_bitcast_fusion
  206.8 8.9 %all-to-all-done.2 = bf16[32,2,2048]{2,1,0:T(2,128)(2,1)S(1)} async-done(((bf16[32,2,2048]{2,1,0:T(2,128)(2,1)}), bf16[32,2,2048]{2,1,0:T(2,128)(2,1)S(1)}, u32[]{:S(2)}, u32[]{:S(2)}) %all-to-all-start.2) | async-done | bytes 262176 | tf_op jit(solution)/shard_map/all_to_all | solution.py:92
  215.8 0.1 reshape.71
  215.9 0.8 convolution_convert_fusion.3
  (1 shorter events, 0.0 us)
Async XLA Ops:
  7.2 119.0 %copy-start = (bf16[1,128,2048]{2,1,0:T(8,128)(2,1)S(1)}, bf16[1,128,2048]{2,1,0:T(8,128)(2,1)}, u32[]{:S(2)}) copy-start(bf16[1,128,2048]{2,1,0:T(8,128)(2,1)} %param.13) | copy-start | bytes 1572868
  7.2 72.6 %copy-start.1 = (bf16[1,2048,128]{2,1,0:T(8,128)(2,1)S(1)}, bf16[1,2048,128]{2,1,0:T(8,128)(2,1)}, u32[]{:S(2)}) copy-start(bf16[1,2048,128]{2,1,0:T(8,128)(2,1)} %param.12) | copy-start | bytes 1572868
  7.2 72.6 %copy-start.2 = (bf16[1,2048,128]{2,1,0:T(8,128)(2,1)S(1)}, bf16[1,2048,128]{2,1,0:T(8,128)(2,1)}, u32[]{:S(2)}) copy-start(bf16[1,2048,128]{2,1,0:T(8,128)(2,1)} %param.11) | copy-start | bytes 1572868
  7.2 72.5 %all-gather.5.cloned.1.call-start = ((), (), s32[]{:S(2)}) async-start(), calls=%async_computation.5 | async-start | bytes 4456448 | tf_op jit(solution)/shard_map/all_gather | solution.py:55
  32.9 93.3 %all-gather.3.cloned.1.call-start = ((), (), s32[]{:S(2)}) async-start(), calls=%async_computation.4 | async-start | bytes 4456448 | tf_op jit(solution)/shard_map/all_gather | solution.py:56
  49.9 144.7 %reduce-scatter.2.cloned.1.call-start = ((), (), s32[]{:S(2)}) async-start(), calls=%async_computation.6 | async-start | bytes 4456448 | tf_op jit(solution)/shard_map/reduce_scatter | solution.py:84
  133.6 1.2 copy-start.4
  134.8 4.1 %copy-start.3 = (bf16[16,64,2048]{2,1,0:T(8,128)(2,1)S(1)}, bf16[16,64,2048]{2,1,0:T(8,128)(2,1)}, u32[]{:S(2)}) copy-start(bf16[16,64,2048]{2,1,0:T(8,128)(2,1)} %all-gather.5.cloned.1.call-done) | copy-start | bytes 12582916
  196.5 19.3 %all-to-all-start.2 = ((bf16[32,2,2048]{2,1,0:T(2,128)(2,1)}), bf16[32,2,2048]{2,1,0:T(2,128)(2,1)S(1)}, u32[]{:S(2)}, u32[]{:S(2)}) async-start(bf16[32,2,2048]{2,1,0:T(2,128)(2,1)} %reshape.70), calls=%async_computation.3 | async-start | bytes 524288 | tf_op jit(solution)/shard_map/all_to_all | solution.py:92
Sparse Core Ops, SparseCore 0:
  33.0 46.7 all-gather.4
  82.4 43.7 all-gather.2
  133.7 60.8 reduce-scatter.1
where the time goes:
time: 227 us; the launch traced here: 223 us
  waiting for transfers between devices  135 us (59%)
  blocking collectives  36.5 us (16%)
  matrix products  20 us (9%)
  between operations  13.8 us (6%)
  starting transfers between devices  9.05 us (4%)
  local copies, waits for them, and re-layouts  7.57 us (3%)
    reduce_scatter x1, waiting for transfers between devices, on_device(): lax.psum_scatter(lax.dot_general(hidden_grads, stacked, (((1,), (1,)), ((...  54.4 us
    all_gather x1, waiting for transfers between devices, on_device(): lax.all_gather(arrived[1].reshape(1, slot_count, model_width), 'dp', axis...  42 us
    all_gather x1, waiting for transfers between devices, on_device(): lax.all_gather(arrived[0].reshape(1, slot_count, model_width), 'dp', axis...  29.8 us
    all_to_all x1, blocking collectives, on_device(): lax.all_to_all(x_slots.reshape(experts, capacity, model_width), 'expert',...  21.5 us
    all_to_all x1, blocking collectives, on_device(): lax.all_to_all(scaled_slots.reshape(experts, capacity, model_width), 'exp...  15 us
    all_to_all x1, waiting for transfers between devices, on_device(): lax.all_to_all(summed.reshape(experts, capacity, model_width), 'expert',...  8.95 us
    all_to_all x1, starting transfers between devices, on_device(): lax.all_to_all(summed.reshape(experts, capacity, model_width), 'expert',...  8.93 us
  transfers between devices with their start and end apart: 4, of which 4 were waited for; matrix products, arithmetic and copies ran while one was open for 6% of the time, Pallas kernels for 0%

commit v1 on v0

v1 whole, which is shorter than its diff:
```python
import jax
import jax.numpy as jnp
from jax import lax
from jax.experimental import pallas as pl
from jax.experimental.pallas import tpu as pltpu
from jax.sharding import PartitionSpec as P

NZ, NY, NX = 8, 8, 4
WIDTH, UNITS = 2048, 128
HALF = WIDTH // 2
F32, BF16 = jnp.float32, jnp.bfloat16
ROWS_T = (((0,), (0,)), ((), ()))
COLS_T = (((1,), (1,)), ((), ()))


def dot(a, b, dims=(((1,), (0,)), ((), ()))):
    return lax.dot_general(a, b, dims, preferred_element_type=F32)


def kernel(
    tok, gout, gw, ids, wg_hbm, wu_hbm, wd_hbm,
    gtok, gwg, gwu, gwd,
    wgu, wd, inf, tyx, tyg, xs, gs, xall, gall, szall, hg, hi, pb, pr, qs, qr, ts, tr, fs, fr,
    w_sem, y_send, y_recv, x_send, x_recv, i_send, i_recv, ring_send, ring_recv,
    sib_send, sib_recv, p_send, p_recv, q_send, q_recv, t_send, t_recv, f_send, f_recv,
):
    dp, ex = lax.axis_index("dp"), lax.axis_index("expert")
    z, c = dp // 2, lax.rem(dp, 2)
    y, x = ex // NX, lax.rem(ex, NX)

    def at_z(k):
        return {"dp": lax.rem(z + k + NZ, NZ) * 2 + c, "expert": ex}

    def at_y(k):
        return {"dp": dp, "expert": lax.rem(y + k, NY) * NX + x}

    def at_x(k):
        return {"dp": dp, "expert": y * NX + lax.rem(x + k, NX)}

    sibling = {"dp": z * 2 + 1 - c, "expert": ex}

    def send(src, dst, ssem, rsem, where):
        copy = pltpu.make_async_remote_copy(
            src_ref=src, dst_ref=dst, send_sem=ssem, recv_sem=rsem,
            device_id=where, device_id_type=pl.DeviceIdType.MESH,
        )
        copy.start()

    def wait(ref, sem):
        pltpu.make_async_copy(ref, ref, sem).wait()

    loads = [
        pltpu.make_async_copy(wg_hbm.at[0], wgu.at[:, pl.ds(0, UNITS)], w_sem.at[0]),
        pltpu.make_async_copy(wu_hbm.at[0], wgu.at[:, pl.ds(UNITS, UNITS)], w_sem.at[1]),
        pltpu.make_async_copy(wd_hbm.at[0], wd, w_sem.at[2]),
    ]
    for load in loads:
        load.start()

    barrier = pltpu.get_barrier_semaphore()
    partners = [at_y(k) for k in range(1, NY)] + [at_x(k) for k in range(1, NX)]
    partners += [at_z(k) for k in range(1, NZ)] + [sibling]
    for partner in partners:
        pl.semaphore_signal(barrier, inc=1, device_id=partner, device_id_type=pl.DeviceIdType.MESH)

    lane = lax.broadcasted_iota(jnp.int32, (8, 128), 1)
    info = jnp.zeros((8, 128), F32)
    for k in range(4):
        info = info + jnp.where(lane == k, ids[:, k : k + 1].astype(F32), 0.0)
        info = info + jnp.where(lane == 4 + k, gw[:, k : k + 1].astype(F32), 0.0)
    inf[y] = jnp.concatenate([info, info], axis=0).astype(BF16)
    t32 = tok[...].astype(F32)
    tyx[y] = jnp.concatenate([t32[:, :HALF], t32[:, HALF:]], axis=0).astype(BF16)
    g32 = gout[...].astype(F32)
    tyg[y] = jnp.concatenate([g32[:, :HALF], g32[:, HALF:]], axis=0).astype(BF16)

    pl.semaphore_wait(barrier, len(partners))

    for n, ref in enumerate((inf, tyx, tyg)):
        for k in range(1, NY):
            send(ref.at[y], ref.at[y], y_send.at[n], y_recv.at[n], at_y(k))

    wait(inf.at[pl.ds(0, NY - 1)], y_recv.at[0])
    table = inf[...].reshape(128, 128).astype(F32)
    r = lax.broadcasted_iota(jnp.int32, (128, 128), 0)
    l = lax.broadcasted_iota(jnp.int32, (128, 128), 1)
    same = ((r // 8) % 2 == l // 64) & (r // 16 == (l // 2) % 8)
    expert = (y * NX + (l // 16) % 4).astype(F32)
    named = jnp.zeros((128, 128), F32)
    weight = jnp.zeros((128, 128), F32)
    for k in range(4):
        match = jnp.where(same & (table[:, k : k + 1] == expert), 1.0, 0.0)
        named = named + match
        weight = weight + match * table[:, 4 + k : 5 + k]
    before = jnp.where((r // 8 == l // 8) & (l < r), 1.0, 0.0).astype(BF16)
    rank = dot(before, named.astype(BF16))
    chosen = jnp.where(rank == (l % 2).astype(F32), named, 0.0)
    member = chosen.astype(BF16)
    weighted = (chosen * weight).astype(BF16)
    szall[z] = member
    for k in range(1, NZ):
        send(szall.at[z], szall.at[z], i_send, i_recv, at_z(k))

    blocks = [[0], [-1, 1], [-2, 2], [-3, 3], [4]]
    number = {0: 0, -1: 1, 1: 2, -2: 3, 2: 4, -3: 5, 3: 6, 4: 7}

    def z_of(o):
        return lax.rem(z + o + NZ, NZ)

    def to_slots(n, ref, table_of, out, whole):
        wait(ref.at[pl.ds(0, NY - 1)], y_recv.at[n + 1])
        rows = dot(table_of, ref[...].reshape(128, HALF), ROWS_T).astype(BF16)
        out[:, :, 0:HALF] = rows[0:64].reshape(NX, 16, HALF)
        out[:, :, HALF:WIDTH] = rows[64:128].reshape(NX, 16, HALF)
        for k in range(1, NX):
            there = lax.rem(x + k, NX)
            send(out.at[there], whole.at[z, c, x], x_send.at[n], x_recv.at[n], at_x(k))
        whole[z, c, x] = out[x]

    def ring(n, whole, s):
        for o in blocks[s]:
            ways = []
            if s == 0:
                wait(xs.at[pl.ds(0, NX - 1)], x_recv.at[n])
                ways = [0, 1]
            else:
                way = n if s == 4 else (0 if o < 0 else 1)
                here = whole.at[z_of(o), c]
                wait(here, ring_recv.at[n, way, s])
                if s < 3 or (s == 3 and way == n):
                    ways = [way]
            here = whole.at[z_of(o), c]
            for way in ways:
                send(here, here, ring_send.at[n, way, s], ring_recv.at[n, way, s + 1],
                     at_z(1 if way == 0 else -1))
            b = number[o]
            send(here, here, sib_send.at[n, b], sib_recv.at[n, b], sibling)

    def compute(o):
        b, zb = number[o], z_of(o)
        wait(xall.at[zb, 1 - c], sib_recv.at[0, b])
        wait(gall.at[zb, 1 - c], sib_recv.at[1, b])
        rows = xall[zb].reshape(128, WIDTH)
        scaled = gall[zb].reshape(128, WIDTH)
        pre = dot(rows, wgu[...])
        grad_hidden = dot(scaled, wd[...], COLS_T)
        gate_pre, up_pre = pre[:, :UNITS], pre[:, UNITS:]
        logistic = jax.nn.sigmoid(gate_pre)
        activated = gate_pre * logistic
        hi[zb] = (activated * up_pre).astype(BF16)
        grad_up = (grad_hidden * activated).astype(BF16)
        grad_gate = (
            grad_hidden * up_pre * (logistic * (1.0 + gate_pre * (1.0 - logistic)))
        ).astype(BF16)
        both = jnp.concatenate([grad_gate, grad_up], axis=1)
        hg[zb] = both
        pb[zb] = dot(both, wgu[...], COLS_T).astype(BF16).reshape(2, 64, WIDTH)
        send(pb.at[zb, 1 - c], pr.at[zb], p_send.at[b], p_recv.at[b], sibling)

    def pair_sum(o):
        b, zb = number[o], z_of(o)
        wait(pr.at[zb], p_recv.at[b])
        total = pb[zb, c].astype(F32) + pr[zb].astype(F32)
        qs[zb] = total.astype(BF16).reshape(NX, 16, WIDTH)
        for k in range(1, NX):
            there = lax.rem(x + k, NX)
            send(qs.at[zb, there], qr.at[zb, x], q_send.at[b], q_recv.at[b], at_x(k))
        qr[zb, x] = qs[zb, x]

    def combine(o):
        b, zb = number[o], z_of(o)
        wait(qr.at[zb, pl.ds(0, NX - 1)], q_recv.at[b])
        slots = qr[zb].reshape(64, WIDTH)
        halves = jnp.concatenate([slots[:, :HALF], slots[:, HALF:]], axis=0)
        ts[zb] = dot(szall[zb], halves).astype(BF16).reshape(NY, 16, HALF)
        for k in range(1, NY):
            there = lax.rem(y + k, NY)
            send(ts.at[zb, there], tr.at[zb, y], t_send.at[b], t_recv.at[b], at_y(k))
        tr[zb, y] = ts[zb, y]

    def y_sum(o):
        b, zb = number[o], z_of(o)
        wait(tr.at[zb, pl.ds(0, NY - 1)], t_recv.at[b])
        total = tr[zb, 0].astype(F32)
        for k in range(1, NY):
            total = total + tr[zb, k].astype(F32)
        fs[zb] = total.astype(BF16)
        if o == 0:
            fr[z] = fs[z]
        else:
            send(fs.at[zb], fr.at[z], f_send, f_recv, at_z(o))

    def weight_grads(first, last):
        def step(j, carry):
            at = pl.ds(pl.multiple_of(j * 256, 256), 256)
            both = hg[...].reshape(1024, 2 * UNITS)
            part = dot(xall[:, :, :, :, at].reshape(1024, 256), both, ROWS_T)
            gwg[0, at, :] = part[:, :UNITS]
            gwu[0, at, :] = part[:, UNITS:]
            hidden = hi[...].reshape(1024, UNITS)
            gwd[0, :, at] = dot(hidden, gall[:, :, :, :, at].reshape(1024, 256), ROWS_T)
            return carry

        lax.fori_loop(first, last, step, 0)

    to_slots(0, tyx, member, xs, xall)
    to_slots(1, tyg, weighted, gs, gall)
    ring(0, xall, 0)
    ring(1, gall, 0)
    for load in loads:
        load.wait()
    compute(0)
    wait(szall.at[pl.ds(0, NZ - 1)], i_recv)
    for s in range(1, 5):
        ring(0, xall, s)
        for o in blocks[s - 1]:
            pair_sum(o)
        for o in blocks[s - 1]:
            combine(o)
        ring(1, gall, s)
        for o in blocks[s]:
            compute(o)
        if s >= 2:
            for o in blocks[s - 2]:
                y_sum(o)
    weight_grads(0, 2)
    pair_sum(4)
    weight_grads(2, 4)
    combine(4)
    for o in blocks[3]:
        y_sum(o)
    weight_grads(4, 8)
    y_sum(4)
    wait(fr.at[pl.ds(0, NZ - 1)], f_recv)
    total = fr[0].astype(F32)
    for k in range(1, NZ):
        total = total + fr[k].astype(F32)
    gtok[:, 0:HALF] = total[0:8].astype(BF16)
    gtok[:, HALF:WIDTH] = total[8:16].astype(BF16)

    for n, ref in enumerate((inf, tyx, tyg)):
        wait(ref.at[pl.ds(0, NY - 1)], y_send.at[n])
    wait(szall.at[pl.ds(0, NZ - 1)], i_send)
    for n, whole in enumerate((xall, gall)):
        wait(xs.at[pl.ds(0, NX - 1)], x_send.at[n])
        for way in range(2):
            for s in range(4 if way == n else 3):
                wait(whole.at[0, 0], ring_send.at[n, way, s])
        for b in range(8):
            wait(whole.at[0, 0], sib_send.at[n, b])
    for b in range(8):
        wait(pr.at[0], p_send.at[b])
        wait(qs.at[0, pl.ds(0, NX - 1)], q_send.at[b])
        wait(ts.at[0, pl.ds(0, NY - 1)], t_send.at[b])
    wait(fs.at[pl.ds(0, NZ - 1)], f_send)


def on_device(tokens, grad_out, gate_weights, expert_ids, w_gate, w_up, w_down):
    vmem = pl.BlockSpec(memory_space=pltpu.VMEM)
    hbm = pl.BlockSpec(memory_space=pl.ANY)
    dma = pltpu.SemaphoreType.DMA
    rows = (NZ, 2, NX, 16, WIDTH)
    scratch = [
        pltpu.VMEM((WIDTH, 2 * UNITS), BF16),
        pltpu.VMEM((UNITS, WIDTH), BF16),
        pltpu.VMEM((NY, 16, 128), BF16),
        pltpu.VMEM((NY, 16, HALF), BF16),
        pltpu.VMEM((NY, 16, HALF), BF16),
        pltpu.VMEM((NX, 16, WIDTH), BF16),
        pltpu.VMEM((NX, 16, WIDTH), BF16),
        pltpu.VMEM(rows, BF16),
        pltpu.VMEM(rows, BF16),
        pltpu.VMEM((NZ, 128, 128), BF16),
        pltpu.VMEM((NZ, 128, 2 * UNITS), BF16),
        pltpu.VMEM((NZ, 128, UNITS), BF16),
        pltpu.VMEM((NZ, 2, 64, WIDTH), BF16),
        pltpu.VMEM((NZ, 64, WIDTH), BF16),
        pltpu.VMEM((NZ, NX, 16, WIDTH), BF16),
        pltpu.VMEM((NZ, NX, 16, WIDTH), BF16),
        pltpu.VMEM((NZ, NY, 16, HALF), BF16),
        pltpu.VMEM((NZ, NY, 16, HALF), BF16),
        pltpu.VMEM((NZ, 16, HALF), BF16),
        pltpu.VMEM((NZ, 16, HALF), BF16),
        dma((3,)),
        dma((3,)),
        dma((3,)),
        dma((2,)),
        dma((2,)),
        dma(()),
        dma(()),
        dma((2, 2, 4)),
        dma((2, 2, 5)),
        dma((2, 8)),
        dma((2, 8)),
        dma((8,)),
        dma((8,)),
        dma((8,)),
        dma((8,)),
        dma((8,)),
        dma((8,)),
        dma(()),
        dma(()),
    ]
    return pl.pallas_call(
        kernel,
        out_shape=(
            jax.ShapeDtypeStruct((8, WIDTH), BF16),
            jax.ShapeDtypeStruct((1, WIDTH, UNITS), F32),
            jax.ShapeDtypeStruct((1, WIDTH, UNITS), F32),
            jax.ShapeDtypeStruct((1, UNITS, WIDTH), F32),
        ),
        in_specs=[vmem, vmem, vmem, vmem, hbm, hbm, hbm],
        out_specs=(vmem, vmem, vmem, vmem),
        scratch_shapes=scratch,
        compiler_params=pltpu.CompilerParams(
            collective_id=0, has_side_effects=True, vmem_limit_bytes=56 * 2**20
        ),
        cost_estimate=pl.CostEstimate(
            flops=4_400_000_000, bytes_accessed=5_000_000, transcendentals=131072
        ),
    )(tokens, grad_out, gate_weights, expert_ids, w_gate, w_up, w_down)


def solution(mesh):
    placed = P(("dp", "expert"), None)
    columns, rows = P("expert", None, "dp"), P("expert", "dp", None)
    return jax.shard_map(
        on_device,
        mesh=mesh,
        in_specs=(placed, placed, placed, placed, columns, columns, rows),
        out_specs=(placed, columns, columns, rows),
        check_vma=False,
    )
```

time: 227 us -> 114 us (0.50); the launches traced: 223 us -> 113 us
  waiting for transfers between devices: 135 us -> 0 us
  Pallas kernels: 0 us -> 104 us
  blocking collectives: 36.5 us -> 0 us
  matrix products: 20 us -> 0 us
  between operations: 13.8 us -> 0.65 us
  starting transfers between devices: 9.05 us -> 0 us
    pallas_call x0 -> x1, Pallas kernels: none -> 104 us  [on_device(): pl.pallas_call(kernel, out_shape=(jax.ShapeDtypeStruct((8, WIDTH), BF16),...]
    all_gather x2 -> x0, waiting for transfers between devices: 71.8 us -> none  [the longest x1 42 us: on_device(): lax.all_gather(arrived[1].reshape(1, slot_count, model_width), 'dp', axis...]
    reduce_scatter x1 -> x0, waiting for transfers between devices: 54.4 us -> none  [on_device(): lax.psum_scatter(lax.dot_general(hidden_grads, stacked, (((1,), (1,)), ((...]
    all_to_all x2 -> x0, blocking collectives: 36.5 us -> none  [the longest x1 21.5 us: on_device(): lax.all_to_all(x_slots.reshape(experts, capacity, model_width), 'expert',...]
    dot_general x8 -> x0, matrix products: 20 us -> none  [the longest x1 4.46 us: on_device(): pre_both = jnp.dot(routed_rows, stacked, preferred_element_type=jnp.float32)]
    all_to_all x1 -> x0, waiting for transfers between devices: 8.95 us -> none  [on_device(): lax.all_to_all(summed.reshape(experts, capacity, model_width), 'expert',...]
    all_to_all x1 -> x0, starting transfers between devices: 8.93 us -> none  [on_device(): lax.all_to_all(summed.reshape(experts, capacity, model_width), 'expert',...]
    unnamed x11 -> x12, local copies, waits for them, and re-layouts: 1.98 us -> 8.32 us
  transfers between devices with their start and end apart: 4 -> 0, of which waited for: 4 -> 0; matrix products, arithmetic and copies ran while one was open for 6% -> 0% of each run, Pallas kernels for 0% -> 0%
where the time goes in v1:
time: 114 us; the launch traced here: 113 us
  Pallas kernels  104 us (91%)
  local copies, waits for them, and re-layouts  8.32 us (7%)
    pallas_call x1, Pallas kernels, on_device(): pl.pallas_call(kernel, out_shape=(jax.ShapeDtypeStruct((8, WIDTH), BF16),...  104 us
    unnamed x12, local copies, waits for them, and re-layouts  8.32 us

profile of v1, /device:TPU:1, one launch (start us, length us, event | category | flops | bytes accessed | tf_op | source)
XLA Modules:
  0.0 113.4 jit_solution(4876162406011244414)
XLA Ops:
  0.6 0.0 copy-start.2
  0.6 1.3 %copy.11.gw = bf16[8,4]{1,0:T(8,128)(2,1)} copy(bf16[8,4]{0,1:T(4,128)(2,1)} %param.9) | data formatting | bytes 128 | tf_op args[2]
  2.0 0.0 copy-done.2
  2.0 0.7 copy.12.ids
  2.7 104.4 %shard_map.102 = (bf16[8,2048]{1,0:T(8,128)(2,1)}, f32[1,2048,128]{2,1,0:T(8,128)}, f32[1,2048,128]{2,1,0:T(8,128)}, f32[1,128,2048]{2,1,0:T(8,128)}) custom-call(bf16[8,2048]{1,0:T(8,128)(2,1)} %tok.1, bf16[8,2048]{1,0:T(8,128)(2,1)} %gout.1, bf16[8,4]{1,0:T(8,128)(2,1)} %copy.11.gw, s32[8,4]{1,0:T(8,128)} %copy.12.ids, bf16[1,2048,128]{2,1,0:T(8,128)(2,1)} %wg_hbm.1, ...), custom_call_target="tpu_custom_call" | custom-call | flops 4400000000 | bytes 5000000 | tf_op jit(solution)/shard_map/pallas_call | solution.py:304
  107.0 1.4 %copy.17 = bf16[8,2048]{1,0:T(8,128)(2,1)} copy(bf16[8,2048]{1,0:T(8,128)(2,1)} %get-tuple-element.8) | data formatting | bytes 65536
  108.4 0.0 copy-start.1
  108.4 2.4 %copy.18 = f32[1,2048,128]{2,1,0:T(8,128)} copy(f32[1,2048,128]{2,1,0:T(8,128)} %get-tuple-element.9) | data formatting | bytes 2097152
  110.8 0.0 copy-done.1
  110.8 0.0 copy-start
  110.8 1.0 copy.19
  111.7 0.6 copy-done
  112.4 1.0 copy.20
Async XLA Ops:
  0.6 1.4 %copy-start.2 = (s32[8,4]{0,1:T(4,128)S(1)}, s32[8,4]{0,1:T(4,128)}, u32[]{:S(2)}) copy-start(s32[8,4]{0,1:T(4,128)} %param.10) | copy-start | bytes 388
  108.4 2.4 %copy-start.1 = (f32[1,2048,128]{2,1,0:T(8,128)S(1)}, f32[1,2048,128]{2,1,0:T(8,128)}, u32[]{:S(2)}) copy-start(f32[1,2048,128]{2,1,0:T(8,128)} %get-tuple-element.10) | copy-start | bytes 3145732
  110.8 1.6 %copy-start = (f32[1,128,2048]{2,1,0:T(8,128)S(1)}, f32[1,128,2048]{2,1,0:T(8,128)}, u32[]{:S(2)}) copy-start(f32[1,128,2048]{2,1,0:T(8,128)} %get-tuple-element.11) | copy-start | bytes 3145732

commit v2 on v1

--- a/solution.py
+++ b/solution.py
@@ -19,10 +19,10 @@
 
 def kernel(
     tok, gout, gw, ids, wg_hbm, wu_hbm, wd_hbm,
-    gtok, gwg, gwu, gwd,
-    wgu, wd, inf, tyx, tyg, xs, gs, xall, gall, szall, hg, hi, pb, pr, qs, qr, ts, tr, fs, fr,
-    w_sem, y_send, y_recv, x_send, x_recv, i_send, i_recv, ring_send, ring_recv,
-    sib_send, sib_recv, p_send, p_recv, q_send, q_recv, t_send, t_recv, f_send, f_recv,
+    gtok, gwg_hbm, gwu_hbm, gwd_hbm,
+    gwg, gwu, gwd, wgu, wd, inf, tyx, tyg, xs, gs, xall, gall, szall, hg, hi, pb, pr, qs, qr, ts, tm, tn, tr, fs, fr,
+    w_sem, o_sem, y_send, y_recv, x_send, x_recv, i_send, i_recv, ring_send, ring_recv,
+    sib_send, sib_recv, p_send, p_recv, q_send, q_recv, m_send, m_recv, t_send, t_recv, f_send, f_recv,
 ):
     dp, ex = lax.axis_index("dp"), lax.axis_index("expert")
     z, c = dp // 2, lax.rem(dp, 2)
@@ -32,7 +32,12 @@
         return {"dp": lax.rem(z + k + NZ, NZ) * 2 + c, "expert": ex}
 
     def at_y(k):
-        return {"dp": dp, "expert": lax.rem(y + k, NY) * NX + x}
+        return {"dp": dp, "expert": lax.rem(y + k + NY, NY) * NX + x}
+
+    way = 1 - 2 * c
+
+    def y_of(k):
+        return lax.rem(y + way * k + NY, NY)
 
     def at_x(k):
         return {"dp": dp, "expert": y * NX + lax.rem(x + k, NX)}
@@ -64,10 +69,14 @@
         pl.semaphore_signal(barrier, inc=1, device_id=partner, device_id_type=pl.DeviceIdType.MESH)
 
     lane = lax.broadcasted_iota(jnp.int32, (8, 128), 1)
+    eye = lax.broadcasted_iota(jnp.int32, (8, 8), 0) == lax.broadcasted_iota(jnp.int32, (8, 8), 1)
+    ids32, gw32 = ids[...].astype(F32), gw[...].astype(F32)
     info = jnp.zeros((8, 128), F32)
-    for k in range(4):
-        info = info + jnp.where(lane == k, ids[:, k : k + 1].astype(F32), 0.0)
-        info = info + jnp.where(lane == 4 + k, gw[:, k : k + 1].astype(F32), 0.0)
+    for n, part in enumerate((ids32, gw32)):
+        for k in range(4):
+            spread = jnp.where(eye, jnp.broadcast_to(part[k : k + 1, :], (8, 8)), 0.0)
+            column = jnp.sum(spread, axis=1, keepdims=True)
+            info = info + jnp.where(lane == 4 * n + k, column, 0.0)
     inf[y] = jnp.concatenate([info, info], axis=0).astype(BF16)
     t32 = tok[...].astype(F32)
     tyx[y] = jnp.concatenate([t32[:, :HALF], t32[:, HALF:]], axis=0).astype(BF16)
@@ -76,9 +85,12 @@
 
     pl.semaphore_wait(barrier, len(partners))
 
-    for n, ref in enumerate((inf, tyx, tyg)):
+    def spread_y(n, ref):
         for k in range(1, NY):
             send(ref.at[y], ref.at[y], y_send.at[n], y_recv.at[n], at_y(k))
+
+    spread_y(0, inf)
+    spread_y(1, tyx)
 
     wait(inf.at[pl.ds(0, NY - 1)], y_recv.at[0])
     table = inf[...].reshape(128, 128).astype(F32)
@@ -109,6 +121,8 @@
 
     def to_slots(n, ref, table_of, out, whole):
         wait(ref.at[pl.ds(0, NY - 1)], y_recv.at[n + 1])
+        if n == 0:
+            spread_y(2, tyg)
         rows = dot(table_of, ref[...].reshape(128, HALF), ROWS_T).astype(BF16)
         out[:, :, 0:HALF] = rows[0:64].reshape(NX, 16, HALF)
         out[:, :, HALF:WIDTH] = rows[64:128].reshape(NX, 16, HALF)
@@ -119,20 +133,20 @@
 
     def ring(n, whole, s):
         for o in blocks[s]:
-            ways = []
+            turns = []
             if s == 0:
                 wait(xs.at[pl.ds(0, NX - 1)], x_recv.at[n])
-                ways = [0, 1]
+                turns = [0, 1]
             else:
-                way = n if s == 4 else (0 if o < 0 else 1)
+                turn = n if s == 4 else (0 if o < 0 else 1)
                 here = whole.at[z_of(o), c]
-                wait(here, ring_recv.at[n, way, s])
-                if s < 3 or (s == 3 and way == n):
-                    ways = [way]
+                wait(here, ring_recv.at[n, turn, s])
+                if s < 3 or (s == 3 and turn == n):
+                    turns = [turn]
             here = whole.at[z_of(o), c]
-            for way in ways:
-                send(here, here, ring_send.at[n, way, s], ring_recv.at[n, way, s + 1],
-                     at_z(1 if way == 0 else -1))
+            for turn in turns:
+                send(here, here, ring_send.at[n, turn, s], ring_recv.at[n, turn, s + 1],
+                     at_z(1 if turn == 0 else -1))
             b = number[o]
             send(here, here, sib_send.at[n, b], sib_recv.at[n, b], sibling)
 
@@ -173,16 +187,26 @@
         slots = qr[zb].reshape(64, WIDTH)
         halves = jnp.concatenate([slots[:, :HALF], slots[:, HALF:]], axis=0)
         ts[zb] = dot(szall[zb], halves).astype(BF16).reshape(NY, 16, HALF)
-        for k in range(1, NY):
-            there = lax.rem(y + k, NY)
-            send(ts.at[zb, there], tr.at[zb, y], t_send.at[b], t_recv.at[b], at_y(k))
-        tr[zb, y] = ts[zb, y]
+        send(ts.at[zb, y_of(-3)], tm.at[zb, 0], m_send.at[b], m_recv.at[b], at_y(-way))
+        send(ts.at[zb, y_of(-4)], tm.at[zb, 1], m_send.at[b], m_recv.at[b], at_y(way))
+        send(ts.at[zb, y_of(-6)], tm.at[zb, 2], m_send.at[b], m_recv.at[b], at_y(way))
+        send(ts.at[zb, y_of(-1)], tr.at[zb, 1], t_send.at[b], t_recv.at[b], at_y(-way))
+        tr[zb, 0] = ts[zb, y]
+
+    def merge(o):
+        b, zb = number[o], z_of(o)
+        wait(tm.at[zb], m_recv.at[b])
+        for n, k in enumerate((2, 5, 7)):
+            there = y_of(-k)
+            total = ts[zb, there].astype(F32) + tm[zb, n].astype(F32)
+            tn[zb, n] = total.astype(BF16)
+            send(tn.at[zb, n], tr.at[zb, 2 + n], t_send.at[b], t_recv.at[b], at_y(-way * k))
 
     def y_sum(o):
         b, zb = number[o], z_of(o)
-        wait(tr.at[zb, pl.ds(0, NY - 1)], t_recv.at[b])
+        wait(tr.at[zb, pl.ds(0, 4)], t_recv.at[b])
         total = tr[zb, 0].astype(F32)
-        for k in range(1, NY):
+        for k in range(1, 5):
             total = total + tr[zb, k].astype(F32)
         fs[zb] = total.astype(BF16)
         if o == 0:
@@ -199,13 +223,16 @@
             gwu[0, at, :] = part[:, UNITS:]
             hidden = hi[...].reshape(1024, UNITS)
             gwd[0, :, at] = dot(hidden, gall[:, :, :, :, at].reshape(1024, 256), ROWS_T)
+            pltpu.make_async_copy(gwg.at[0, at], gwg_hbm.at[0, at], o_sem.at[0]).start()
+            pltpu.make_async_copy(gwu.at[0, at], gwu_hbm.at[0, at], o_sem.at[1]).start()
+            pltpu.make_async_copy(gwd.at[0, :, at], gwd_hbm.at[0, :, at], o_sem.at[2]).start()
             return carry
 
         lax.fori_loop(first, last, step, 0)
 
     to_slots(0, tyx, member, xs, xall)
+    ring(0, xall, 0)
     to_slots(1, tyg, weighted, gs, gall)
-    ring(0, xall, 0)
     ring(1, gall, 0)
     for load in loads:
         load.wait()
@@ -215,22 +242,32 @@
         ring(0, xall, s)
         for o in blocks[s - 1]:
             pair_sum(o)
-        for o in blocks[s - 1]:
-            combine(o)
+        if s >= 2:
+            for o in blocks[s - 2]:
+                merge(o)
         ring(1, gall, s)
+        if s < 4:
+            for o in blocks[s - 1]:
+                combine(o)
         for o in blocks[s]:
             compute(o)
         if s >= 2:
             for o in blocks[s - 2]:
                 y_sum(o)
+    for o in blocks[3]:
+        combine(o)
+    pair_sum(4)
     weight_grads(0, 2)
-    pair_sum(4)
+    for o in blocks[3]:
+        merge(o)
+    combine(4)
     weight_grads(2, 4)
-    combine(4)
+    merge(4)
     for o in blocks[3]:
         y_sum(o)
-    weight_grads(4, 8)
+    weight_grads(4, 7)
     y_sum(4)
+    weight_grads(7, 8)
     wait(fr.at[pl.ds(0, NZ - 1)], f_recv)
     total = fr[0].astype(F32)
     for k in range(1, NZ):
@@ -243,16 +280,40 @@
     wait(szall.at[pl.ds(0, NZ - 1)], i_send)
     for n, whole in enumerate((xall, gall)):
         wait(xs.at[pl.ds(0, NX - 1)], x_send.at[n])
-        for way in range(2):
-            for s in range(4 if way == n else 3):
-                wait(whole.at[0, 0], ring_send.at[n, way, s])
+        for turn in range(2):
+            for s in range(4 if turn == n else 3):
+                wait(whole.at[0, 0], ring_send.at[n, turn, s])
         for b in range(8):
             wait(whole.at[0, 0], sib_send.at[n, b])
     for b in range(8):
         wait(pr.at[0], p_send.at[b])
         wait(qs.at[0, pl.ds(0, NX - 1)], q_send.at[b])
-        wait(ts.at[0, pl.ds(0, NY - 1)], t_send.at[b])
+        wait(tm.at[0], m_send.at[b])
+        wait(tr.at[0, pl.ds(0, 4)], t_send.at[b])
     wait(fs.at[pl.ds(0, NZ - 1)], f_send)
+    for n, ref in enumerate((gwg, gwu, gwd)):
+        wait(ref, o_sem.at[n])
+
+
+def hand_over(tok, gate, up, down, tok_out, gate_out, up_out, down_out, *scratch):
+    held, in_sem, out_sem = scratch[:4], scratch[4], scratch[5]
+    pieces = []
+    for k in range(4):
+        for n, extent in ((1, WIDTH), (2, WIDTH), (3, UNITS)):
+            pieces.append((n, (0, pl.ds(k * extent // 4, extent // 4))))
+    pieces.append((0, (pl.ds(0, 8),)))
+    ins, outs = (tok, gate, up, down), (tok_out, gate_out, up_out, down_out)
+    loads, stores = [], []
+    for m, (n, at) in enumerate(pieces):
+        loads.append(pltpu.make_async_copy(ins[n].at[at], held[n].at[at], in_sem.at[m]))
+        stores.append(pltpu.make_async_copy(held[n].at[at], outs[n].at[at], out_sem.at[m]))
+    for load in loads:
+        load.start()
+    for load, store in zip(loads, stores):
+        load.wait()
+        store.start()
+    for store in stores:
+        store.wait()
 
 
 def on_device(tokens, grad_out, gate_weights, expert_ids, w_gate, w_up, w_down):
@@ -261,6 +322,9 @@
     dma = pltpu.SemaphoreType.DMA
     rows = (NZ, 2, NX, 16, WIDTH)
     scratch = [
+        pltpu.VMEM((1, WIDTH, UNITS), F32),
+        pltpu.VMEM((1, WIDTH, UNITS), F32),
+        pltpu.VMEM((1, UNITS, WIDTH), F32),
         pltpu.VMEM((WIDTH, 2 * UNITS), BF16),
         pltpu.VMEM((UNITS, WIDTH), BF16),
         pltpu.VMEM((NY, 16, 128), BF16),
@@ -278,9 +342,12 @@
         pltpu.VMEM((NZ, NX, 16, WIDTH), BF16),
         pltpu.VMEM((NZ, NX, 16, WIDTH), BF16),
         pltpu.VMEM((NZ, NY, 16, HALF), BF16),
-        pltpu.VMEM((NZ, NY, 16, HALF), BF16),
+        pltpu.VMEM((NZ, 3, 16, HALF), BF16),
+        pltpu.VMEM((NZ, 3, 16, HALF), BF16),
+        pltpu.VMEM((NZ, 5, 16, HALF), BF16),
         pltpu.VMEM((NZ, 16, HALF), BF16),
         pltpu.VMEM((NZ, 16, HALF), BF16),
+        dma((3,)),
         dma((3,)),
         dma((3,)),
         dma((3,)),
@@ -298,10 +365,12 @@
         dma((8,)),
         dma((8,)),
         dma((8,)),
+        dma((8,)),
+        dma((8,)),
         dma(()),
         dma(()),
     ]
-    return pl.pallas_call(
+    outs = pl.pallas_call(
         kernel,
         out_shape=(
             jax.ShapeDtypeStruct((8, WIDTH), BF16),
@@ -310,7 +379,7 @@
             jax.ShapeDtypeStruct((1, UNITS, WIDTH), F32),
         ),
         in_specs=[vmem, vmem, vmem, vmem, hbm, hbm, hbm],
-        out_specs=(vmem, vmem, vmem, vmem),
+        out_specs=(vmem, hbm, hbm, hbm),
         scratch_shapes=scratch,
         compiler_params=pltpu.CompilerParams(
             collective_id=0, has_side_effects=True, vmem_limit_bytes=56 * 2**20
@@ -318,7 +387,15 @@
         cost_estimate=pl.CostEstimate(
             flops=4_400_000_000, bytes_accessed=5_000_000, transcendentals=131072
         ),
-    )(tokens, grad_out, gate_weights, expert_ids, w_gate, w_up, w_down)
+    )(tokens, grad_out, gate_weights.T, expert_ids.T, w_gate, w_up, w_down)
+    return pl.pallas_call(
+        hand_over,
+        out_shape=tuple(jax.ShapeDtypeStruct(out.shape, out.dtype) for out in outs),
+        in_specs=[hbm] * 4,
+        out_specs=(hbm,) * 4,
+        scratch_shapes=[pltpu.VMEM(out.shape, out.dtype) for out in outs] + [dma((13,)), dma((13,))],
+        compiler_params=pltpu.CompilerParams(vmem_limit_bytes=56 * 2**20),
+    )(*outs)
 
 
 def solution(mesh):

time: 114 us -> 104 us (0.912)
  local copies, waits for them, and re-layouts: 8.32 us -> 0 us
    unnamed x12 -> x0, local copies, waits for them, and re-layouts: 8.32 us -> none
    pallas_call x1, Pallas kernels: 104 us -> 101 us  [on_device(): pl.pallas_call(kernel, out_shape=(jax.ShapeDtypeStruct((8, WIDTH), BF16),...]
    pallas_call x0 -> x1, Pallas kernels: none -> 2.83 us  [on_device(): pl.pallas_call(hand_over, out_shape=tuple((jax.ShapeDtypeStruct(out.shape...]
where the time goes in v2:
time: 104 us
  Pallas kernels  103 us (99%)
    pallas_call x1, Pallas kernels, on_device(): pl.pallas_call(kernel, out_shape=(jax.ShapeDtypeStruct((8, WIDTH), BF16),...  101 us
    pallas_call x1, Pallas kernels, on_device(): pl.pallas_call(hand_over, out_shape=tuple((jax.ShapeDtypeStruct(out.shape...  2.83 us

profile of v2, /device:TPU:1, one launch (start us, length us, event | category | flops | bytes accessed | tf_op | source)
XLA Modules:
  0.0 104.1 jit_solution(6270895388904934571)
XLA Ops:
  0.6 100.6 %shard_map.102 = (bf16[8,2048]{1,0:T(8,128)(2,1)}, f32[1,2048,128]{2,1,0:T(8,128)}, f32[1,2048,128]{2,1,0:T(8,128)}, f32[1,128,2048]{2,1,0:T(8,128)}) custom-call(bf16[8,2048]{1,0:T(8,128)(2,1)} %tok.1, bf16[8,2048]{1,0:T(8,128)(2,1)} %gout.1, bf16[4,8]{1,0:T(4,128)(2,1)} %bitcast.3, s32[4,8]{1,0:T(4,128)} %bitcast.2, bf16[1,2048,128]{2,1,0:T(8,128)(2,1)} %wg_hbm.1, ...), custom_call_target="tpu_custom_call" | custom-call | flops 4400000000 | bytes 5000000 | tf_op jit(solution)/shard_map/pallas_call | solution.py:373
  101.2 2.8 %shard_map.103 = (bf16[8,2048]{1,0:T(8,128)(2,1)}, f32[1,2048,128]{2,1,0:T(8,128)}, f32[1,2048,128]{2,1,0:T(8,128)}, f32[1,128,2048]{2,1,0:T(8,128)}) custom-call(bf16[8,2048]{1,0:T(8,128)(2,1)} %get-tuple-element.8.tok, f32[1,2048,128]{2,1,0:T(8,128)} %get-tuple-element.9.gate, f32[1,2048,128]{2,1,0:T(8,128)} %get-tuple-element.10.up, ...), custom_call_target="tpu_custom_call" | custom-call | tf_op jit(solution)/shard_map/pallas_call | solution.py:391

commit v3 on v2

--- a/solution.py
+++ b/solution.py
@@ -10,7 +10,6 @@
 HALF = WIDTH // 2
 F32, BF16 = jnp.float32, jnp.bfloat16
 ROWS_T = (((0,), (0,)), ((), ()))
-COLS_T = (((1,), (1,)), ((), ()))
 
 
 def dot(a, b, dims=(((1,), (0,)), ((), ()))):
@@ -20,7 +19,7 @@
 def kernel(
     tok, gout, gw, ids, wg_hbm, wu_hbm, wd_hbm,
     gtok, gwg_hbm, gwu_hbm, gwd_hbm,
-    gwg, gwu, gwd, wgu, wd, inf, tyx, tyg, xs, gs, xall, gall, szall, hg, hi, pb, pr, qs, qr, ts, tm, tn, tr, fs, fr,
+    gwg, gwu, gwd, wgu, wd, wgu_t, wd_t, inf, tyx, tyg, xs, gs, xall, gall, szall, hg, hi, pb, pr, qs, qr, ts, tm, tn, tr, last, fs, fr,
     w_sem, o_sem, y_send, y_recv, x_send, x_recv, i_send, i_recv, ring_send, ring_recv,
     sib_send, sib_recv, p_send, p_recv, q_send, q_recv, m_send, m_recv, t_send, t_recv, f_send, f_recv,
 ):
@@ -113,6 +112,11 @@
     for k in range(1, NZ):
         send(szall.at[z], szall.at[z], i_send, i_recv, at_z(k))
 
+    for load in loads:
+        load.wait()
+    wgu_t[...] = wgu[...].T
+    wd_t[...] = wd[...].T
+
     blocks = [[0], [-1, 1], [-2, 2], [-3, 3], [4]]
     number = {0: 0, -1: 1, 1: 2, -2: 3, 2: 4, -3: 5, 3: 6, 4: 7}
 
@@ -157,7 +161,7 @@
         rows = xall[zb].reshape(128, WIDTH)
         scaled = gall[zb].reshape(128, WIDTH)
         pre = dot(rows, wgu[...])
-        grad_hidden = dot(scaled, wd[...], COLS_T)
+        grad_hidden = dot(scaled, wd_t[...])
         gate_pre, up_pre = pre[:, :UNITS], pre[:, UNITS:]
         logistic = jax.nn.sigmoid(gate_pre)
         activated = gate_pre * logistic
@@ -168,7 +172,7 @@
         ).astype(BF16)
         both = jnp.concatenate([grad_gate, grad_up], axis=1)
         hg[zb] = both
-        pb[zb] = dot(both, wgu[...], COLS_T).astype(BF16).reshape(2, 64, WIDTH)
+        pb[zb] = dot(both, wgu_t[...]).astype(BF16).reshape(2, 64, WIDTH)
         send(pb.at[zb, 1 - c], pr.at[zb], p_send.at[b], p_recv.at[b], sibling)
 
     def pair_sum(o):
@@ -187,6 +191,12 @@
         slots = qr[zb].reshape(64, WIDTH)
         halves = jnp.concatenate([slots[:, :HALF], slots[:, HALF:]], axis=0)
         ts[zb] = dot(szall[zb], halves).astype(BF16).reshape(NY, 16, HALF)
+        if o == 4:
+            for k in range(1, NY):
+                there = lax.rem(y + k, NY)
+                send(ts.at[zb, there], last.at[y], t_send.at[b], t_recv.at[b], at_y(k))
+            last[y] = ts[zb, y]
+            return
         send(ts.at[zb, y_of(-3)], tm.at[zb, 0], m_send.at[b], m_recv.at[b], at_y(-way))
         send(ts.at[zb, y_of(-4)], tm.at[zb, 1], m_send.at[b], m_recv.at[b], at_y(way))
         send(ts.at[zb, y_of(-6)], tm.at[zb, 2], m_send.at[b], m_recv.at[b], at_y(way))
@@ -204,10 +214,12 @@
 
     def y_sum(o):
         b, zb = number[o], z_of(o)
-        wait(tr.at[zb, pl.ds(0, 4)], t_recv.at[b])
-        total = tr[zb, 0].astype(F32)
-        for k in range(1, 5):
-            total = total + tr[zb, k].astype(F32)
+        parts = last if o == 4 else tr.at[zb]
+        count = parts.shape[0]
+        wait(parts.at[pl.ds(0, count - 1)], t_recv.at[b])
+        total = parts[0].astype(F32)
+        for k in range(1, count):
+            total = total + parts[k].astype(F32)
         fs[zb] = total.astype(BF16)
         if o == 0:
             fr[z] = fs[z]
@@ -234,8 +246,6 @@
     ring(0, xall, 0)
     to_slots(1, tyg, weighted, gs, gall)
     ring(1, gall, 0)
-    for load in loads:
-        load.wait()
     compute(0)
     wait(szall.at[pl.ds(0, NZ - 1)], i_recv)
     for s in range(1, 5):
@@ -246,35 +256,22 @@
             for o in blocks[s - 2]:
                 merge(o)
         ring(1, gall, s)
-        if s < 4:
-            for o in blocks[s - 1]:
-                combine(o)
         for o in blocks[s]:
             compute(o)
+        for o in blocks[s - 1]:
+            combine(o)
         if s >= 2:
             for o in blocks[s - 2]:
                 y_sum(o)
-    for o in blocks[3]:
-        combine(o)
     pair_sum(4)
     weight_grads(0, 2)
     for o in blocks[3]:
         merge(o)
     combine(4)
     weight_grads(2, 4)
-    merge(4)
     for o in blocks[3]:
         y_sum(o)
     weight_grads(4, 7)
-    y_sum(4)
-    weight_grads(7, 8)
-    wait(fr.at[pl.ds(0, NZ - 1)], f_recv)
-    total = fr[0].astype(F32)
-    for k in range(1, NZ):
-        total = total + fr[k].astype(F32)
-    gtok[:, 0:HALF] = total[0:8].astype(BF16)
-    gtok[:, HALF:WIDTH] = total[8:16].astype(BF16)
-
     for n, ref in enumerate((inf, tyx, tyg)):
         wait(ref.at[pl.ds(0, NY - 1)], y_send.at[n])
     wait(szall.at[pl.ds(0, NZ - 1)], i_send)
@@ -288,8 +285,19 @@
     for b in range(8):
         wait(pr.at[0], p_send.at[b])
         wait(qs.at[0, pl.ds(0, NX - 1)], q_send.at[b])
-        wait(tm.at[0], m_send.at[b])
-        wait(tr.at[0, pl.ds(0, 4)], t_send.at[b])
+        if b < 7:
+            wait(tm.at[0], m_send.at[b])
+    y_sum(4)
+    weight_grads(7, 8)
+    wait(fr.at[pl.ds(0, NZ - 1)], f_recv)
+    total = fr[0].astype(F32)
+    for k in range(1, NZ):
+        total = total + fr[k].astype(F32)
+    gtok[:, 0:HALF] = total[0:8].astype(BF16)
+    gtok[:, HALF:WIDTH] = total[8:16].astype(BF16)
+
+    for b in range(8):
+        wait(last.at[pl.ds(0, 7)] if b == 7 else tr.at[0, pl.ds(0, 4)], t_send.at[b])
     wait(fs.at[pl.ds(0, NZ - 1)], f_send)
     for n, ref in enumerate((gwg, gwu, gwd)):
         wait(ref, o_sem.at[n])
@@ -327,6 +335,8 @@
         pltpu.VMEM((1, UNITS, WIDTH), F32),
         pltpu.VMEM((WIDTH, 2 * UNITS), BF16),
         pltpu.VMEM((UNITS, WIDTH), BF16),
+        pltpu.VMEM((2 * UNITS, WIDTH), BF16),
+        pltpu.VMEM((WIDTH, UNITS), BF16),
         pltpu.VMEM((NY, 16, 128), BF16),
         pltpu.VMEM((NY, 16, HALF), BF16),
         pltpu.VMEM((NY, 16, HALF), BF16),
@@ -345,6 +355,7 @@
         pltpu.VMEM((NZ, 3, 16, HALF), BF16),
         pltpu.VMEM((NZ, 3, 16, HALF), BF16),
         pltpu.VMEM((NZ, 5, 16, HALF), BF16),
+        pltpu.VMEM((NY, 16, HALF), BF16),
         pltpu.VMEM((NZ, 16, HALF), BF16),
         pltpu.VMEM((NZ, 16, HALF), BF16),
         dma((3,)),

time: 104 us -> 105 us (level)
  the two profiles are of different devices: /device:TPU:1 before, /device:TPU:16 now
where the time goes in v3:
time: 105 us
  Pallas kernels  104 us (99%)
    pallas_call x1, Pallas kernels, on_device(): pl.pallas_call(kernel, out_shape=(jax.ShapeDtypeStruct((8, WIDTH), BF16),...  102 us
    pallas_call x1, Pallas kernels, on_device(): pl.pallas_call(hand_over, out_shape=tuple((jax.ShapeDtypeStruct(out.shape...  2.83 us

profile of v3, /device:TPU:16, one launch (start us, length us, event | category | flops | bytes accessed | tf_op | source)
XLA Modules:
  0.0 105.0 jit_solution(761639120696423341)
XLA Ops:
  0.6 101.5 %shard_map.102 = (bf16[8,2048]{1,0:T(8,128)(2,1)}, f32[1,2048,128]{2,1,0:T(8,128)}, f32[1,2048,128]{2,1,0:T(8,128)}, f32[1,128,2048]{2,1,0:T(8,128)}) custom-call(bf16[8,2048]{1,0:T(8,128)(2,1)} %tok.1, bf16[8,2048]{1,0:T(8,128)(2,1)} %gout.1, bf16[4,8]{1,0:T(4,128)(2,1)} %bitcast.3, s32[4,8]{1,0:T(4,128)} %bitcast.2, bf16[1,2048,128]{2,1,0:T(8,128)(2,1)} %wg_hbm.1, ...), custom_call_target="tpu_custom_call" | custom-call | flops 4400000000 | bytes 5000000 | tf_op jit(solution)/shard_map/pallas_call | solution.py:384
  102.1 2.8 %shard_map.103 = (bf16[8,2048]{1,0:T(8,128)(2,1)}, f32[1,2048,128]{2,1,0:T(8,128)}, f32[1,2048,128]{2,1,0:T(8,128)}, f32[1,128,2048]{2,1,0:T(8,128)}) custom-call(bf16[8,2048]{1,0:T(8,128)(2,1)} %get-tuple-element.8.tok, f32[1,2048,128]{2,1,0:T(8,128)} %get-tuple-element.9.gate, f32[1,2048,128]{2,1,0:T(8,128)} %get-tuple-element.10.up, ...), custom_call_target="tpu_custom_call" | custom-call | tf_op jit(solution)/shard_map/pallas_call | solution.py:402
